TPU v7x, 32 devices: a whole 2x2x4 slice. The times are simulated.
32 devices in a mesh: seq: 8 (over z, y), head: 4 (over x, core).
Axes of the slice: x: 2, y: 2, z: 4, core: 2. Of those that a mesh axis runs over, the one named last changes fastest.
Arguments:
- hidden_in: bfloat16 [16384, 1536], P('seq'), may hold values from -6 to 6
- norm_gain: float32 [1536], replicated, may hold values from 0.5 to 1.5
- w_z: bfloat16 [1536, 3072], P(None, 'head'), may hold values from -0.15625 to 0.15625
- w_x: bfloat16 [1536, 3072], P(None, 'head'), may hold values from -0.15625 to 0.15625
- w_bc: bfloat16 [1536, 2, 128], P(None, None, 'head'), may hold values from -0.15625 to 0.15625
- w_dt: bfloat16 [1536, 48], P(None, 'head'), may hold values from -0.15625 to 0.15625
- conv_x: float32 [4, 3072], P(None, 'head'), may hold values from -3 to 3
- conv_x_bias: float32 [3072], P('head'), may hold values from -1.8 to 1.8
- conv_bc: float32 [4, 2, 128], P(None, None, 'head'), may hold values from -3 to 3
- conv_bc_bias: float32 [2, 128], P(None, 'head'), may hold values from -1.8 to 1.8
- dt_bias: float32 [48], P('head'), may hold values from -1.5 to 0.5
- a_log: float32 [48], P('head'), may hold values from -9 to -3.5
- d_skip: float32 [48], P('head'), may hold values from 0.5 to 1.5
- gate_gain: float32 [3072], P('head'), may hold values from 0.5 to 1.5
- w_out: bfloat16 [3072, 1536], P('head'), may hold values from -0.109375 to 0.109375
- out_grad: bfloat16 [16384, 1536], P(('seq', 'head')), may hold values from -6 to 6
Outputs:
- output: bfloat16 [16384, 1536], P(('seq', 'head'))
- input_grad: float32 [16384, 1536], P(('seq', 'head'))
- norm_gain_grad: float32 [1536], replicated
- w_z_grad: float32 [1536, 3072], P(None, 'head')
- w_x_grad: float32 [1536, 3072], P(None, 'head')
- w_bc_grad: float32 [1536, 2, 128], P(None, None, 'head')
- w_dt_grad: float32 [1536, 48], P(None, 'head')
- conv_x_grad: float32 [4, 3072], P(None, 'head')
- conv_x_bias_grad: float32 [3072], P('head')
- conv_bc_grad: float32 [4, 2, 128], P(None, None, 'head')
- conv_bc_bias_grad: float32 [2, 128], P(None, 'head')
- dt_bias_grad: float32 [48], P('head')
- a_log_grad: float32 [48], P('head')
- d_skip_grad: float32 [48], P('head')
- gate_gain_grad: float32 [3072], P('head')
- w_out_grad: float32 [3072, 1536], P('head')
All inputs are finite; a program needn't handle non-finite values.
Results may differ from a plain program's by a relative error of at most 0.038.
Values may be sent and summed in bfloat16 or wider, within the bound.
A program may use at most 192 MiB of HBM per device.

v0:
```python
import jax
import jax.numpy as jnp
from jax import lax
from jax.sharding import PartitionSpec as P

INNER = 3072
HEAD_DIM = 64
CONV = 4
BLOCK = 256


EPSILON = 1e-05
HIGHEST = lax.Precision.HIGHEST


def from_behind(value, axis, by):
    size = lax.axis_size(axis)
    pairs = [(i, i + by) for i in range(size) if 0 <= i + by < size]
    return lax.ppermute(value, axis, pairs)


def prefix(value, axis, join, neutral, backward):
    count, mine = (lax.axis_size(axis), lax.axis_index(axis))
    pieces = jax.tree.map(lambda part: lax.all_gather(part, axis), value)
    if backward:
        pieces = jax.tree.map(lambda part: part[::-1], pieces)
        mine = count - 1 - mine
    so_far = jax.tree.map(
        lambda part, zero: jnp.full_like(part, 0) + jnp.asarray(zero, part.dtype), value, neutral
    )

    def lap(position, so_far):
        longer = join(so_far, jax.tree.map(lambda part: part[position], pieces))
        return jax.tree.map(lambda new, old: jnp.where(position < mine, new, old), longer, so_far)

    return lax.fori_loop(0, count - 1, lap, so_far)


def block_scan(state, values, keys_b, queries_c, widths, a_log):
    count = values.shape[0] // BLOCK

    def advance(carry, pieces):
        vals, keys, queries, steps = pieces
        decay = steps * -jnp.exp(a_log)
        cumul = jnp.cumsum(decay, axis=0)
        causal = (
            lax.broadcasted_iota(jnp.int32, (BLOCK, BLOCK), 0)
            >= lax.broadcasted_iota(jnp.int32, (BLOCK, BLOCK), 1)
        )[:, :, None]
        spread = cumul[:, None, :] - cumul[None, :, :]
        weights = jnp.where(causal, jnp.exp(jnp.where(causal, spread, 0.0)), 0.0)
        scores = jnp.dot(queries, keys.T, precision=HIGHEST)
        mixing = scores[:, :, None] * weights * steps[None, :, :]
        result = jnp.einsum("tsh,shp->thp", mixing, vals, precision=HIGHEST)
        result = result + jnp.exp(cumul)[:, :, None] * jnp.einsum(
            "tn,hpn->thp", queries, carry, precision=HIGHEST
        )
        tail = jnp.exp(cumul[-1][None, :] - cumul) * steps
        carry = jnp.exp(cumul[-1])[:, None, None] * carry + jnp.einsum(
            "sh,shp,sn->hpn", tail, vals, keys, precision=HIGHEST
        )
        return (carry, result)

    pieces = (
        values.reshape((count, BLOCK) + values.shape[1:]),
        keys_b.reshape((count, BLOCK) + keys_b.shape[1:]),
        queries_c.reshape((count, BLOCK) + queries_c.shape[1:]),
        widths.reshape((count, BLOCK) + widths.shape[1:]),
    )
    final, results = lax.scan(jax.checkpoint(advance), state, pieces)
    return (final, results.reshape(values.shape))


def norm_rows(rows_in, gain):
    return rows_in * lax.rsqrt(jnp.mean(rows_in * rows_in, -1, keepdims=True) + EPSILON) * gain


def conv_silu(padded_x, padded_bc, kernel_x, bias_x, kernel_bc, bias_bc):
    length = padded_x.shape[0] - (CONV - 1)
    total_x = bias_x + kernel_x[0] * padded_x[0:length]
    total_bc = bias_bc + kernel_bc[0] * padded_bc[0:length]
    for offset in range(1, CONV):
        total_x = total_x + kernel_x[offset] * padded_x[offset : offset + length]
        total_bc = total_bc + kernel_bc[offset] * padded_bc[offset : offset + length]
    return (jax.nn.silu(total_x), jax.nn.silu(total_bc))


def block_state(values, keys_b, widths_raw, dt_bias, a_log):
    steps = jax.nn.softplus(widths_raw + dt_bias)
    decay = steps * -jnp.exp(a_log)
    cumul = jnp.cumsum(decay, axis=0)
    total = cumul[-1]
    weights = jnp.exp(total[None, :] - cumul) * steps
    local_state = jnp.einsum("th,thp,tn->hpn", weights, values, keys_b, precision=HIGHEST)
    return (jnp.exp(total), local_state)


def mixer(state_in, values, keys_b, queries_c, widths_raw, dt_bias, a_log, d_skip):
    steps = jax.nn.softplus(widths_raw + dt_bias)
    final, results = block_scan(state_in, values, keys_b, queries_c, steps, a_log)
    results = results + d_skip[None, :, None] * values
    return (results.reshape(values.shape[0], -1), final)


def gate_silu(mixed, gate_in):
    return mixed * jax.nn.silu(gate_in)


def chain_pair(earlier, later):
    return (earlier[0] * later[0], later[1] + later[0][:, None, None] * earlier[1])


def times_transposed(left, right):
    return lax.dot_general(
        left, right, (((1,), (1,)), ((), ())), preferred_element_type=jnp.float32
    )


def transposed_times(left, right):
    return lax.dot_general(
        left, right, (((0,), (0,)), ((), ())), preferred_element_type=jnp.float32
    )


def per_device(
    hidden_in,
    norm_gain,
    w_z,
    w_x,
    w_bc,
    w_dt,
    conv_x,
    conv_x_bias,
    conv_bc,
    conv_bc_bias,
    dt_bias,
    a_log,
    d_skip,
    gate_gain,
    w_out,
    out_grad,
):
    tokens = hidden_in.shape[0]
    own_rows = out_grad.shape[0]
    heads_here = w_dt.shape[1]
    inner_here = w_z.shape[1]
    edge = CONV - 1
    first_row = lax.axis_index("head") * own_rows
    hidden_f = hidden_in.astype(jnp.float32)
    normed_in = norm_rows(hidden_f, norm_gain).astype(jnp.bfloat16)
    proj_z = jnp.dot(normed_in, w_z, preferred_element_type=jnp.float32).astype(jnp.bfloat16)
    proj_x = jnp.dot(normed_in, w_x, preferred_element_type=jnp.float32).astype(jnp.bfloat16)
    proj_bc = jnp.einsum("td,dkn->tkn", normed_in, w_bc, preferred_element_type=jnp.float32).astype(
        jnp.bfloat16
    )
    proj_dt = jnp.dot(normed_in, w_dt, preferred_element_type=jnp.float32).astype(jnp.bfloat16)
    edge_x, edge_bc = from_behind((proj_x[-edge:], proj_bc[-edge:]), "seq", 1)
    padded_x = jnp.concatenate([edge_x, proj_x], 0).astype(jnp.float32)
    padded_bc = jnp.concatenate([edge_bc, proj_bc], 0).astype(jnp.float32)
    (inner_act, bc_act), conv_back = jax.vjp(
        conv_silu, padded_x, padded_bc, conv_x, conv_x_bias, conv_bc, conv_bc_bias
    )
    inner_low = inner_act.astype(jnp.bfloat16)
    bc_low = bc_act.astype(jnp.bfloat16)
    bc_whole = lax.all_gather(bc_low, "head", axis=2, tiled=True)
    values = inner_low.astype(jnp.float32).reshape(tokens, heads_here, HEAD_DIM)
    keys_b = bc_whole[:, 0].astype(jnp.float32)
    queries_c = bc_whole[:, 1].astype(jnp.float32)
    widths_raw = proj_dt.astype(jnp.float32)
    (decay_total, state_local), state_back = jax.vjp(
        block_state, values, keys_b, widths_raw, dt_bias, a_log
    )
    identity = (jnp.ones_like(decay_total), jnp.zeros_like(state_local))
    state_in = prefix((decay_total, state_local), "seq", chain_pair, identity, False)[1]
    (mixed, final_state), mixer_back = jax.vjp(
        mixer, state_in, values, keys_b, queries_c, widths_raw, dt_bias, a_log, d_skip
    )
    gated, gate_back = jax.vjp(gate_silu, mixed, proj_z.astype(jnp.float32))
    squares = lax.psum(jnp.sum(gated * gated, -1), "head")
    inverse = lax.rsqrt(squares / INNER + EPSILON)
    normed_out = (gated * inverse[:, None] * gate_gain).astype(jnp.bfloat16)
    out_part = lax.psum_scatter(
        jnp.dot(normed_out, w_out, preferred_element_type=jnp.float32),
        "head",
        scatter_dimension=0,
        tiled=True,
    )
    hidden_own = lax.dynamic_slice_in_dim(hidden_f, first_row, own_rows, 0)
    output = (hidden_own + out_part).astype(jnp.bfloat16)
    piece = lax.all_gather(out_grad, "head", axis=0, tiled=True)
    part = times_transposed(piece, w_out)
    d_normed = part
    d_normed, w_out_grad = (d_normed, transposed_times(normed_out, piece))
    weighted = d_normed * gate_gain
    row_dots = lax.psum(jnp.sum(weighted * gated, -1), "head")
    d_gated = (
        weighted * inverse[:, None]
        - gated * (inverse * inverse * inverse * row_dots / INNER)[:, None]
    )
    gate_gain_grad = jnp.sum(d_normed * gated * inverse[:, None], 0)
    d_mixed, d_gate_z = gate_back(d_gated)
    d_state_in, d_values_a, d_keys_a, d_queries, d_widths_a, d_bias_a, d_alog_a, d_skip_grad = (
        mixer_back((d_mixed, jnp.zeros_like(final_state)))
    )
    state_out_grad = prefix((decay_total, d_state_in), "seq", chain_pair, identity, True)[1]
    d_values_b, d_keys_b, d_widths_b, d_bias_b, d_alog_b = state_back(
        (jnp.sum(state_out_grad * state_in, (1, 2)), state_out_grad)
    )
    d_inner = (d_values_a + d_values_b).reshape(tokens, inner_here)
    d_bc_whole = jnp.stack([d_keys_a + d_keys_b, d_queries], 1)
    d_bc_own = lax.psum_scatter(d_bc_whole, "head", scatter_dimension=2, tiled=True)
    d_pad_x, d_pad_bc, conv_x_grad, conv_x_bias_grad, conv_bc_grad, conv_bc_bias_grad = conv_back(
        (d_inner, d_bc_own)
    )
    back_x, back_bc = from_behind((d_pad_x[:edge], d_pad_bc[:edge]), "seq", -1)
    grad_x = jnp.concatenate([d_pad_x[edge:-edge], d_pad_x[-edge:] + back_x], 0).astype(
        jnp.bfloat16
    )
    grad_bc = jnp.concatenate([d_pad_bc[edge:-edge], d_pad_bc[-edge:] + back_bc], 0).astype(
        jnp.bfloat16
    )
    grad_z = d_gate_z.astype(jnp.bfloat16)
    grad_dt = (d_widths_a + d_widths_b).astype(jnp.bfloat16)
    w_z_grad = transposed_times(normed_in, grad_z)
    w_x_grad = transposed_times(normed_in, grad_x)
    w_bc_grad = jnp.einsum("td,tkn->dkn", normed_in, grad_bc, preferred_element_type=jnp.float32)
    w_dt_grad = transposed_times(normed_in, grad_dt)
    part = times_transposed(grad_z, w_z)
    part = part + times_transposed(grad_x, w_x)
    part = part + jnp.einsum("tkn,dkn->td", grad_bc, w_bc, preferred_element_type=jnp.float32)
    d_normed_rows = lax.psum_scatter(
        part + times_transposed(grad_dt, w_dt), "head", scatter_dimension=0, tiled=True
    )
    _, norm_back = jax.vjp(norm_rows, hidden_own, norm_gain)
    input_rows, gain_part = norm_back(d_normed_rows)
    norm_gain_grad = lax.psum(gain_part, "head")
    input_grad = input_rows + out_grad.astype(jnp.float32)
    summed = lax.psum(
        (
            norm_gain_grad,
            w_z_grad,
            w_x_grad,
            w_bc_grad,
            w_dt_grad,
            conv_x_grad,
            conv_x_bias_grad,
            conv_bc_grad,
            conv_bc_bias_grad,
            d_bias_a + d_bias_b,
            d_alog_a + d_alog_b,
            d_skip_grad,
            gate_gain_grad,
            w_out_grad,
        ),
        "seq",
    )
    return (output, input_grad) + tuple(summed)


def solution(mesh):
    placed = (
        P("seq", None),
        P(),
        P(None, "head"),
        P(None, "head"),
        P(None, None, "head"),
        P(None, "head"),
        P(None, "head"),
        P("head"),
        P(None, None, "head"),
        P(None, "head"),
        P("head"),
        P("head"),
        P("head"),
        P("head"),
        P("head", None),
        P(("seq", "head"), None),
    )
    return jax.shard_map(
        per_device,
        mesh=mesh,
        in_specs=placed,
        out_specs=(
            P(("seq", "head"), None),
            P(("seq", "head"), None),
            P(),
            P(None, "head"),
            P(None, "head"),
            P(None, None, "head"),
            P(None, "head"),
            P(None, "head"),
            P("head"),
            P(None, None, "head"),
            P(None, "head"),
            P("head"),
            P("head"),
            P("head"),
            P("head"),
            P("head", None),
        ),
        check_vma=False,
    )
```

profile of v0, /device:TPU:0, one launch (start us, length us, event | category | flops | bytes accessed | tf_op | source)
XLA Modules:
  0.0 2153.3 jit_solution(10793594368419147208)
XLA Ops:
  13.5 8.9 convolution_convert_fusion.1
  67.3 20.5 all-gather.2
  112.4 14.1 all-gather.12.cloned.1.call-done
  126.5 8.1 while.72
  138.8 267.0 %while.71 = (s32[]{:T(128)}, f32[12,64,128]{2,1,0:T(8,128)S(1)}, f32[8,256,12,64]{1,0,3,2:T(8,128)}, f32[8,12,64,128]{3,2,1,0:T(8,128)}, f32[8,256,12]{1,2,0:T(8...) while((s32[]{:T(128)}, f32[12,64,128]{2,1,0:T(8,128)S(1)}, ...), condition=%wide.region_8.10_spmd.clone.clone, body=%wide.region_5.9_spmd.clone.clone.sunk | while | flops 1313743872 | bytes 10507149 | solution.py:70
  150.1 18.6 dynamic_update_slice.70
  183.5 18.5 dynamic_update_slice.70
  216.8 18.5 dynamic_update_slice.70
  250.2 18.5 dynamic_update_slice.70
  283.5 18.5 dynamic_update_slice.70
  316.9 18.5 dynamic_update_slice.70
  350.2 18.5 dynamic_update_slice.70
  383.6 18.5 dynamic_update_slice.70
  405.8 8.5 copy.344
  420.9 13.1 multiply_reduce_fusion.11
  440.2 11.5 multiply_reduce_fusion.4
  458.1 15.2 multiply_reduce_fusion.5
  479.8 8.5 copy.345
  494.3 778.6 %while.73 = (s32[]{:T(128)}, f32[12]{0:T(128)}, f32[12,64,128]{2,1,0:T(8,128)}, f32[8,256,12,64]{1,0,3,2:T(8,128)}, f32[8,256,128]{2,1,0:T(8,128)}, /*index=5*/f...) while((s32[]{:T(128)}, f32[12]{0:T(128)}, ...), condition=%wide.region_27.29_spmd.clone, body=%wide.region_14.28_spmd.clone.sunk | while | flops 3038789632 | bytes 27541364 | solution.py:70
  566.0 18.5 dynamic_update_slice.73
  663.4 18.5 dynamic_update_slice.73
  760.8 18.5 dynamic_update_slice.73
  822.7 6.9 fusion.259
  858.1 18.5 dynamic_update_slice.73
  955.5 18.5 dynamic_update_slice.73
  1017.4 6.9 fusion.259
  1052.9 18.5 dynamic_update_slice.73
  1150.3 18.5 dynamic_update_slice.73
  1212.2 6.9 fusion.259
  1247.7 18.5 dynamic_update_slice.73
  1273.7 7.2 reshape.360
  1286.0 10.0 fusion.145
  1296.0 36.1 %all-gather.14.cloned.1.call-done = f32[96,64,128]{2,1,0:T(8,128)} async-done(((f32[12,64,128]{2,1,0:T(8,128)}), f32[96,64,128]{2,1,0:T(8,128)}) %all-gather.14.cloned.1.call-update) | async-done | bytes 3145744 | tf_op jit(solution)/shard_map/all_gather | solution.py:24
  1336.1 8.0 while.74
  1344.1 9.2 multiply_add_fusion
  1367.6 18.3 multiply_reduce_fusion.9
  1400.1 14.9 reduce-window.80
  1416.1 8.2 fusion.146
  1434.6 8.1 fusion.110
  1451.4 17.7 fusion.87
  1469.8 12.1 fusion.134
  1482.2 11.2 fusion.147
  1493.4 10.9 fusion.133
  1515.0 9.2 convert_element_type.70
  1526.8 42.5 %reduce-scatter.8.cloned.1.call-done = f32[512,1536]{1,0:T(8,128)} async-done(((f32[2048,1536]{1,0:T(8,128)}), f32[512,1536]{1,0:T(8,128)}) %reduce-scatter.8.cloned.1.call-update) | async-done | bytes 3145744 | tf_op jit(solution)/shard_map/reduce_scatter | solution.py:231
  1578.8 38.4 %all-reduce.19 = (f32[1536]{0:T(1024)}, f32[4,768]{1,0:T(4,128)}, f32[768]{0:T(1024)}, f32[4,2,32]{2,1,0:T(2,128)}, f32[2,32]{1,0:T(2,128)}, /*index=5*/f32[12]{...) all-reduce(f32[1536]{0:T(1024)S(1)} %psum.121, ...), channel_id=1, replica_groups=mesh['seq'=8,'head'=4] {'seq'}, use_global_device_ids=true, to_apply=%region_40.42 | all-reduce | flops 6500 | bytes 52000 | tf_op jit(solution)/shard_map/psum | solution.py:238
  1617.2 54.0 %reduce-scatter.4.cloned.1.call-done = f32[512,1536]{1,0:T(8,128)} async-done(((f32[2048,1536]{1,0:T(8,128)}), f32[512,1536]{1,0:T(8,128)}) %reduce-scatter.4.cloned.1.call-update) | async-done | bytes 3145744 | tf_op jit(solution)/shard_map/reduce_scatter | solution.py:182
  1678.0 456.4 %all-reduce.23.cloned.1.call-done = (f32[1536,768]{1,0:T(8,128)}, f32[1536,768]{1,0:T(8,128)}, f32[1536,2,32]{0,2,1:T(8,128)}, f32[1536,12]{0,1:T(8,128)}, f32[768,1536]{1,0:T(8,128)}) async-done(((f32[1536,768]{1,0:T(8,128)}, f32[1536,768]{1,0:T(8,128)}, f32[1536,2,32]{0,2,1:T(8,128)}, f32[1536,12]{0,1:T(8,128)}, f32[768,1536]{1,0:T(8,128)}), (f32[1536,768]{1,0:T(8,128)}, f32[1536,768]{1,0:T(8,128)}, ...) | async-done | bytes 14622736 | tf_op jit(solution)/shard_map/psum | solution.py:238
  (1071 shorter events, 953.0 us)
Async XLA Ops:
  7.2 413.7 %copy-start = (bf16[1536,768]{1,0:T(8,128)(2,1)S(1)}, bf16[1536,768]{1,0:T(8,128)(2,1)}, u32[]{:S(2)}) copy-start(bf16[1536,768]{1,0:T(8,128)(2,1)} %param.27) | copy-start | bytes 7077892
  7.2 52.6 %all-gather.8.cloned.1.call-start = ((), (), s32[]{:S(2)}) async-start(), calls=%async_computation.3 | async-start | bytes 1310720 | tf_op jit(solution)/shard_map/all_gather | solution.py:165
  13.5 20.1 copy-start.3
  13.5 14.0 copy-start.36
  22.4 13.0 copy-start.22
  22.4 11.2 copy-start.40
  22.5 20.5 collective-permute-start
  29.5 11.8 copy-start.85
  29.6 10.7 collective-permute-start.1
  40.2 19.6 copy-start.32
  42.7 83.7 %all-gather.12.cloned.1.call-start = ((), (), s32[]{:S(2)}) async-start(), calls=%async_computation.8 | async-start | bytes 3538944 | tf_op jit(solution)/shard_map/all_gather | solution.py:24
  51.8 36.8 %copy-start.82 = (f32[12]{0:T(128)S(1)}, f32[12]{0:T(128)}, u32[]{:S(2)}) copy-start(f32[12]{0:T(128)} %param.37) | copy-start | bytes 148
  65.8 374.3 %all-gather.10.cloned.1.call-start = ((), (), s32[]{:S(2)}) async-start(), calls=%async_computation.5 | async-start | bytes 7864320 | tf_op jit(solution)/shard_map/all_gather | solution.py:190
  66.6 1265.5 %all-gather.14.cloned.1.call-start = ((), (), s32[]{:S(2)}) async-start(), calls=%async_computation.9 | async-start | bytes 3538944 | tf_op jit(solution)/shard_map/all_gather | solution.py:24
  420.9 19.3 copy-start.78
  440.2 17.9 copy-start.56
  504.6 17.2 copy-start.14
  601.0 18.2 copy-start.14
  698.4 18.2 copy-start.14
  795.7 18.2 copy-start.14
  893.1 18.2 copy-start.14
  990.5 18.2 copy-start.14
  1087.9 18.2 copy-start.14
  1185.3 18.2 copy-start.14
  1273.0 169.7 %reduce-scatter.6.cloned.1.call-start = ((), (), s32[]{:S(2)}) async-start(), calls=%async_computation.6 | async-start | bytes 2621440 | tf_op jit(solution)/shard_map/reduce_scatter | solution.py:211
  1273.7 12.2 copy-start.39
  1296.0 48.1 %copy-start.26 = (bf16[2048,2,128]{0,2,1:T(8,128)(2,1)S(1)}, bf16[2048,2,128]{0,2,1:T(8,128)(2,1)}, u32[]{:S(2)}) copy-start(bf16[2048,2,128]{0,2,1:T(8,128)(2,1)} %all-gather.8.cloned.1.call-done) | copy-start | bytes 3145732
  1296.0 48.1 %copy-start.33 = (f32[2048,12]{0,1:T(8,128)S(1)}, f32[2048,12]{0,1:T(8,128)}, u32[]{:S(2)}) copy-start(f32[2048,12]{0,1:T(8,128)} %copy-done.32) | copy-start | bytes 294916
  1296.0 48.1 %copy-start.83 = (f32[12]{0:T(128)S(1)}, f32[12]{0:T(128)}, u32[]{:S(2)}) copy-start(f32[12]{0:T(128)} %param.37) | copy-start | bytes 148
  1353.3 12.6 copy-start.18
  1367.5 201.8 %reduce-scatter.8.cloned.1.call-start = ((), (), s32[]{:S(2)}) async-start(), calls=%async_computation.7 | async-start | bytes 15728640 | tf_op jit(solution)/shard_map/reduce_scatter | solution.py:231
  1367.5 18.3 copy-start.49
  1367.6 18.3 copy-start.51
  1367.6 18.3 copy-start.53
  1367.6 18.3 copy-start.55
  1391.4 24.1 %copy-start.76 = (f32[12]{0:T(128)S(1)}, f32[12]{0:T(128)}, u32[]{:S(2)}) copy-start(f32[12]{0:T(128)} %copy-done.75) | copy-start | bytes 148
  1391.5 24.6 %copy-start.41 = (bf16[1536,12]{0,1:T(8,128)(2,1)S(1)}, bf16[1536,12]{0,1:T(8,128)(2,1)}, u32[]{:S(2)}) copy-start(bf16[1536,12]{0,1:T(8,128)(2,1)} %param.30) | copy-start | bytes 110596
  1398.0 33.8 %collective-permute-start.2 = (f32[3,768]{1,0:T(4,128)S(1)}, f32[3,768]{1,0:T(4,128)S(1)}, u32[]{:S(2)}, u32[]{:S(2)}) collective-permute-start(f32[3,768]{1,0:T(4,128)S(1)} %pad_add_fusion.4), channel_id=1, source_target_pairs={{4,0},{8,4},{12,8},{16,12},{20,16},{24,20},{28,24},{5,1},{9,5},{13... | collective-permute-start | bytes 27656 | tf_op jit(solution)/shard_map/ppermute | solution.py:19
  1444.8 6.4 collective-permute-start.3
  1469.1 202.0 %reduce-scatter.4.cloned.1.call-start = ((), (), s32[]{:S(2)}) async-start(), calls=%async_computation.4 | async-start | bytes 15728640 | tf_op jit(solution)/shard_map/reduce_scatter | solution.py:182
  1481.9 652.5 %all-reduce.23.cloned.1.call-start = ((), (), s32[]{:S(2)}) async-start(), calls=%async_computation.10 | async-start | bytes 29294592 | tf_op jit(solution)/shard_map/psum | solution.py:238
  1482.2 22.1 %slice-start = ((s8[6291456]{0:T(1024)(128)(4,1)}), s8[4194304]{0:T(1024)(128)(4,1)S(1)}, s32[]{:S(2)}) async-start(s8[6291456]{0:T(1024)(128)(4,1)} %bitcast.417), calls=%async_computation.11 | async-start | bytes 8388608
  1515.0 11.5 copy-start.61
  1515.0 11.8 copy-start.59
  1515.0 11.8 copy-start.60
  1515.0 54.3 %copy-start.45 = (f32[1536]{0:T(1024)S(1)}, f32[1536]{0:T(1024)}, u32[]{:S(2)}) copy-start(f32[1536]{0:T(1024)} %param.26) | copy-start | bytes 18436
  1524.2 54.6 %copy-start.80 = (f32[768]{0:T(1024)S(1)}, f32[768]{0:T(1024)}, u32[]{:S(2)}) copy-start(f32[768]{0:T(1024)} %get-tuple-element.919) | copy-start | bytes 9220
  1524.2 147.0 %copy-start.15 = (bf16[512,1536]{1,0:T(8,128)(2,1)S(1)}, bf16[512,1536]{1,0:T(8,128)(2,1)}, u32[]{:S(2)}) copy-start(bf16[512,1536]{1,0:T(8,128)(2,1)} %param.40) | copy-start | bytes 4718596
  (129 other events, 718.4 us)
Sparse Core Ops, SparseCore 0:
  42.8 16.9 all-gather.7
  66.0 60.4 all-gather.11
  128.0 45.0 all-gather.9
  1273.1 58.9 all-gather.13
  1367.6 30.0 reduce-scatter.5
  1469.2 99.9 reduce-scatter.7
  1572.0 99.0 reduce-scatter.3
  1678.4 455.9 all-reduce.22
where the time goes:
time: 2180 us; the launch traced here: 2150 us
  local copies, waits for them, and re-layouts  662 us (30%)
  waiting for transfers between devices  612 us (28%)
  matrix products  464 us (21%)
  other arithmetic  308 us (14%)
  blocking collectives  77.2 us (4%)
    psum x1, waiting for transfers between devices, per_device(): lax.psum((norm_gain_grad, w_z_grad, w_x_grad, w_bc_grad, w_dt_grad, conv_...  456 us
    dynamic_update_slice x56, local copies, waits for them, and re-layouts, block_scan(): final, results = lax.scan(jax.checkpoint(advance), state, pieces)  341 us
    dot_general x24, matrix products, advance(): result = jnp.einsum('tsh,shp->thp', mixing, vals, precision=HIGHEST)  129 us
    another operation x104, other arithmetic  121 us
    another operation x129, local copies, waits for them, and re-layouts  86.6 us
    dot_general x32, matrix products, advance(): jnp.einsum('tn,hpn->thp', queries, carry, precision=HIGHEST)  67.3 us
    dot_general x24, matrix products, advance(): jnp.einsum('sh,shp,sn->hpn', tail, vals, keys, precision=HIGHEST)  64.8 us
    unnamed x192, local copies, waits for them, and re-layouts  58.7 us
  transfers between devices with their start and end apart: 12, of which 7 were waited for; matrix products, arithmetic and copies ran while one was open for 23% of the time, Pallas kernels for 0%

commit v1 on v0

v1 whole, which is shorter than its diff:
```python
import functools

import jax
import jax.numpy as jnp
from jax import lax
from jax.experimental import pallas as pl
from jax.experimental.pallas import tpu as pltpu
from jax.sharding import PartitionSpec as P

INNER = 3072
HEAD_DIM = 64
CONV = 4
STATE = 128
LANES = 128
CHUNK = 256
HALF = 128
EPSILON = 1e-05
F32 = jnp.float32
BF16 = jnp.bfloat16
VMEM_LIMIT = 56 * 1024 * 1024


def dot(left, right, contract=((1,), (0,)), precision=None):
    return lax.dot_general(
        left, right, (contract, ((), ())), preferred_element_type=F32, precision=precision
    )


NT = ((1,), (1,))
TN = ((0,), (0,))


def spread(per_head, expander):
    high = per_head.astype(BF16)
    low = (per_head - high.astype(F32)).astype(BF16)
    return dot(high, expander) + dot(low, expander)


def gather_heads(wide, expander):
    high = wide.astype(BF16)
    low = (wide - high.astype(F32)).astype(BF16)
    return dot(high, expander, NT) + dot(low, expander, NT)


def triangle(rows, lower):
    row = lax.broadcasted_iota(jnp.int32, (rows, rows), 0)
    column = lax.broadcasted_iota(jnp.int32, (rows, rows), 1)
    return row >= column if lower else row <= column


def split_pair(pair):
    first = lax.broadcasted_iota(jnp.int32, pair.shape, 1) < HEAD_DIM
    zero = jnp.zeros_like(pair)
    return jnp.where(first, pair, zero), jnp.where(first, zero, pair)


def sigmoid(value):
    return 0.5 * jnp.tanh(0.5 * value) + 0.5


def convolve(padded, taps, bias, lanes):
    total = bias[:, lanes] + taps[0:1, lanes] * padded[pl.ds(5, CHUNK), lanes]
    for tap in range(1, CONV):
        total = total + taps[tap : tap + 1, lanes] * padded[pl.ds(5 + tap, CHUNK), lanes]
    return total


def slabs(width):
    return [pl.ds(start, LANES) for start in range(0, width, LANES)]


def local_state_kernel(
    x_raw, bc_raw, dt_raw, edge_x, edge_bc, conv_x, bias_x, conv_bc, bias_bc, dt_bias, rate, expander,
    x_act, bc_act, dt_out, cumul_out, packed, padded_x, padded_bc, state, total,
):
    step = pl.program_id(0)
    inner = x_raw.shape[1]

    @pl.when(step == 0)
    def _():
        padded_x[0:8] = edge_x[...].astype(F32)
        padded_bc[0:8] = edge_bc[...].astype(F32)
        state[...] = jnp.zeros_like(state)
        total[...] = jnp.zeros_like(total)

    @pl.when(step > 0)
    def _():
        padded_x[0:8] = padded_x[CHUNK : CHUNK + 8]
        padded_bc[0:8] = padded_bc[CHUNK : CHUNK + 8]

    padded_x[8:] = x_raw[...].astype(F32)
    padded_bc[8:] = bc_raw[...].astype(F32)
    for lanes in slabs(2 * STATE):
        conv = convolve(padded_bc, conv_bc, bias_bc, lanes)
        bc_act[:, lanes] = (conv * sigmoid(conv)).astype(BF16)
    steps = jax.nn.softplus(dt_raw[...].astype(F32) + dt_bias[...])
    cumul = dot(
        triangle(CHUNK, True).astype(F32), steps * rate[...], precision=lax.Precision.HIGHEST
    )
    dt_out[...] = steps
    cumul_out[...] = cumul
    last = cumul[CHUNK - 1 : CHUNK]
    tail = spread(steps * jnp.exp(last - cumul), expander[...])
    keys = bc_act[:, 0:STATE]
    decay = spread(jnp.exp(jnp.broadcast_to(last, (8, LANES))), expander[...])[0:1]
    for index, lanes in enumerate(slabs(inner)):
        conv = convolve(padded_x, conv_x, bias_x, lanes)
        act = (conv * sigmoid(conv)).astype(BF16)
        x_act[:, lanes] = act
        cut = slice(index * LANES, (index + 1) * LANES)
        weighted = (act.astype(F32) * tail[:, cut]).astype(BF16)
        state[:, lanes] = decay[:, cut] * state[:, lanes] + dot(keys, weighted, TN)
    total[...] += last

    @pl.when(step == pl.num_programs(0) - 1)
    def _():
        packed[0:STATE] = state[...].astype(BF16)
        whole = spread(jnp.broadcast_to(total[...], (16, LANES)), expander[...])
        high = whole.astype(BF16)
        low = (whole - high.astype(F32)).astype(BF16)
        row = lax.broadcasted_iota(jnp.int32, whole.shape, 0)
        packed[STATE : STATE + 16] = jnp.where(row == 0, high, low)


def forward_kernel(
    x_act, bc_act, dt_in, cumul_in, gate, d_normed, state_in, skip, gain, expander,
    mixed_out, sums, states, state, scores, mixing, squares, dots,
):
    step = pl.program_id(0)
    inner = x_act.shape[1]

    @pl.when(step == 0)
    def _():
        state[...] = state_in[...]

    states[0] = state[...].astype(BF16)
    keys, queries = bc_act[:, 0:STATE], bc_act[:, STATE : 2 * STATE]
    steps, cumul = dt_in[...], cumul_in[...]
    turned = cumul.T
    last = cumul[CHUNK - 1 : CHUNK]
    raw = dot(queries, keys, NT)
    keep = triangle(HALF, True)
    scores[0] = jnp.where(keep, raw[0:HALF, 0:HALF], 0.0)
    scores[1] = raw[HALF:, 0:HALF]
    scores[2] = jnp.where(keep, raw[HALF:, HALF:], 0.0)
    steps_wide = spread(steps, expander[...])
    tail = spread(jnp.exp(last - cumul), expander[...])
    reach = spread(jnp.exp(cumul), expander[...])
    decay = spread(jnp.exp(jnp.broadcast_to(last, (8, LANES))), expander[...])[0:1]
    for index, lanes in enumerate(slabs(inner)):
        cut = slice(index * LANES, (index + 1) * LANES)
        act = x_act[:, lanes].astype(F32)
        scaled = act * steps_wide[:, cut]
        low = scaled.astype(BF16)
        pair = split_pair(low)
        for part in range(2):
            head = 2 * index + part
            column = cumul[:, head : head + 1]
            row = turned[head : head + 1]
            base = part * CHUNK
            for block, (at, source) in enumerate(((0, 0), (1, 0), (1, 1))):
                gap = column[at * HALF : (at + 1) * HALF] - row[:, source * HALF : (source + 1) * HALF]
                weight = (scores[block] * jnp.exp(jnp.minimum(gap, 0.0))).astype(BF16)
                if at == 0:
                    mixing[0:HALF, part * HALF : (part + 1) * HALF] = weight
                else:
                    mixing[HALF:, base + source * HALF : base + (source + 1) * HALF] = weight
        upper = dot(
            mixing[0:HALF, 0:CHUNK], jnp.concatenate([pair[0][0:HALF], pair[1][0:HALF]], 0)
        )
        lower = dot(mixing[HALF:, :], jnp.concatenate([pair[0], pair[1]], 0))
        held = state[:, lanes]
        carried = dot(queries, held.astype(BF16)) * reach[:, cut]
        mixed = jnp.concatenate([upper, lower], 0) + carried + skip[:, lanes] * act
        state[:, lanes] = decay[:, cut] * held + dot(keys, (scaled * tail[:, cut]).astype(BF16), TN)
        mixed_low = mixed.astype(BF16)
        mixed_out[:, lanes] = mixed_low
        z = gate[:, lanes].astype(F32)
        gated = mixed_low.astype(F32) * (z * sigmoid(z))
        grad = d_normed[:, lanes].astype(F32) * gain[:, lanes]
        if index == 0:
            squares[...] = gated * gated
            dots[...] = gated * grad
        else:
            squares[...] += gated * gated
            dots[...] += gated * grad
    lane = lax.broadcasted_iota(jnp.int32, (CHUNK, LANES), 1)
    sums[...] = jnp.where(
        lane == 0,
        jnp.sum(squares[...], 1, keepdims=True),
        jnp.where(lane == 1, jnp.sum(dots[...], 1, keepdims=True), 0.0),
    )


def gate_kernel(
    mixed_in, gate, d_normed, sums, bc_act, cumul_in, gain, expander,
    normed_out, d_mixed, d_gate, gain_grad, packed, adjoint, gain_total,
):
    step = pl.program_id(0)
    inner = mixed_in.shape[1]

    @pl.when(step == 0)
    def _():
        adjoint[...] = jnp.zeros_like(adjoint)
        gain_total[...] = jnp.zeros_like(gain_total)

    queries = bc_act[:, STATE : 2 * STATE]
    cumul = cumul_in[...]
    last = cumul[CHUNK - 1 : CHUNK]
    reach = spread(jnp.exp(cumul), expander[...])
    decay = spread(jnp.exp(jnp.broadcast_to(last, (8, LANES))), expander[...])[0:1]
    inverse = lax.rsqrt(sums[:, 0:1] / INNER + EPSILON)
    factor = inverse * inverse * inverse * sums[:, 1:2] / INNER
    inverse = jnp.broadcast_to(inverse, (CHUNK, LANES))
    factor = jnp.broadcast_to(factor, (CHUNK, LANES))
    for index, lanes in enumerate(slabs(inner)):
        cut = slice(index * LANES, (index + 1) * LANES)
        mixed = mixed_in[:, lanes].astype(F32)
        z = gate[:, lanes].astype(F32)
        soft = sigmoid(z)
        silu = z * soft
        gated = mixed * silu
        scaled = d_normed[:, lanes].astype(F32) * inverse
        normed = gated * inverse
        normed_out[:, lanes] = (normed * gain[:, lanes]).astype(BF16)
        gain_total[0:1, lanes] += jnp.sum(scaled * gated, 0, keepdims=True)
        d_gated = scaled * gain[:, lanes] - gated * factor
        d_y = (d_gated * silu).astype(BF16)
        d_mixed[:, lanes] = d_y
        d_gate[:, lanes] = (d_gated * mixed * (soft + silu * (1.0 - soft))).astype(BF16)
        reached = (d_y.astype(F32) * reach[:, cut]).astype(BF16)
        adjoint[:, lanes] = decay[:, cut] * adjoint[:, lanes] + dot(queries, reached, TN)

    @pl.when(step == pl.num_programs(0) - 1)
    def _():
        packed[...] = adjoint[...].astype(BF16)
        gain_grad[...] = gain_total[...]


def backward_kernel(
    x_raw, x_before, bc_raw, bc_before, dt_raw, edge_x, edge_bc, bc_act, dt_in, cumul_in, mixed_in, d_mixed,
    states, final_state, adjoint_in, conv_x, bias_x, conv_bc, bias_bc, dt_bias, rate, skip, skip_heads, expander,
    d_x_raw, d_bc_raw, d_dt_raw, first_x, first_bc, conv_x_grad, conv_bc_grad, head_grads,
    padded_x, padded_bc, later_x, later_bc, adjoint, next_state, scores, mixing, d_scores,
    d_steps_total, d_cumul_total,
):
    step = pl.program_id(0)
    steps_here = pl.num_programs(0)
    inner = x_raw.shape[1]

    @pl.when(step == 0)
    def _():
        adjoint[...] = adjoint_in[...]
        next_state[...] = final_state[...]
        later_x[CHUNK : CHUNK + 8] = jnp.zeros((8, inner), F32)
        later_bc[CHUNK : CHUNK + 8] = jnp.zeros((8, 2 * STATE), F32)
        conv_x_grad[...] = jnp.zeros_like(conv_x_grad)
        conv_bc_grad[...] = jnp.zeros_like(conv_bc_grad)
        head_grads[...] = jnp.zeros_like(head_grads)

    @pl.when(step > 0)
    def _():
        later_x[CHUNK : CHUNK + 8] = later_x[0:8]
        later_bc[CHUNK : CHUNK + 8] = later_bc[0:8]

    @pl.when(step == steps_here - 1)
    def _():
        padded_x[0:8] = edge_x[...].astype(F32)
        padded_bc[0:8] = edge_bc[...].astype(F32)

    @pl.when(step < steps_here - 1)
    def _():
        padded_x[0:8] = x_before[...].astype(F32)[8:16]
        padded_bc[0:8] = bc_before[...].astype(F32)[8:16]

    padded_x[8:] = x_raw[...].astype(F32)
    padded_bc[8:] = bc_raw[...].astype(F32)

    keys, queries = bc_act[:, 0:STATE], bc_act[:, STATE : 2 * STATE]
    steps, cumul = dt_in[...], cumul_in[...]
    turned = cumul.T
    last = cumul[CHUNK - 1 : CHUNK]
    raw = dot(keys, queries, NT)
    keep = triangle(HALF, False)
    scores[0] = jnp.where(keep, raw[0:HALF, 0:HALF], 0.0)
    scores[1] = raw[0:HALF, HALF:]
    scores[2] = jnp.where(keep, raw[HALF:, HALF:], 0.0)
    d_scores[...] = jnp.zeros_like(d_scores)
    steps_wide = spread(steps, expander[...])
    tail = spread(jnp.exp(last - cumul), expander[...])
    reach = spread(jnp.exp(cumul), expander[...])
    decay = spread(jnp.exp(jnp.broadcast_to(last, (8, LANES))), expander[...])[0:1]
    d_keys = jnp.zeros((CHUNK, STATE), F32)
    d_queries = jnp.zeros((CHUNK, STATE), F32)
    d_steps = jnp.zeros((CHUNK, LANES), F32)
    d_mix_sum = jnp.zeros((CHUNK, LANES), F32)
    d_skip_sum = jnp.zeros((CHUNK, LANES), F32)
    ending = jnp.zeros((8, LANES), F32)
    for index, lanes in enumerate(slabs(inner)):
        cut = slice(index * LANES, (index + 1) * LANES)
        expand = expander[:, lanes]
        conv = convolve(padded_x, conv_x, bias_x, lanes)
        soft = sigmoid(conv)
        act = (conv * soft).astype(BF16).astype(F32)
        scaled = act * steps_wide[:, cut]
        low = scaled.astype(BF16)
        pair = split_pair(low)
        d_y_low = d_mixed[:, lanes]
        d_y = d_y_low.astype(F32)
        d_pair = split_pair(d_y_low)
        for part in range(2):
            head = 2 * index + part
            column = cumul[:, head : head + 1]
            row = turned[head : head + 1]
            base = part * CHUNK
            d_mixing = dot(pair[part], d_y_low, NT)
            for block, (source, at) in enumerate(((0, 0), (0, 1), (1, 1))):
                gap = row[:, at * HALF : (at + 1) * HALF] - column[source * HALF : (source + 1) * HALF]
                fade = jnp.exp(jnp.minimum(gap, 0.0))
                weight = (scores[block] * fade).astype(BF16)
                d_scores[block] += fade * d_mixing[
                    source * HALF : (source + 1) * HALF, at * HALF : (at + 1) * HALF
                ]
                if source == 0:
                    mixing[0:HALF, base + at * HALF : base + (at + 1) * HALF] = weight
                else:
                    mixing[HALF:, part * HALF : (part + 1) * HALF] = weight
        upper = dot(mixing[0:HALF, :], jnp.concatenate([d_pair[0], d_pair[1]], 0))
        lower = dot(
            mixing[HALF:, 0:CHUNK], jnp.concatenate([d_pair[0][HALF:], d_pair[1][HALF:]], 0)
        )
        after = adjoint[:, lanes]
        after_low = after.astype(BF16)
        before_low = states[0, :, lanes]
        u = jnp.concatenate([upper, lower], 0) + dot(keys, after_low) * tail[:, cut]
        d_act = steps_wide[:, cut] * u + skip[:, lanes] * d_y
        d_steps += gather_heads(act * u, expand)
        d_mix_sum += gather_heads(d_y * mixed_in[:, lanes].astype(F32), expand)
        d_skip_sum += gather_heads(d_y * act, expand)
        closing = jnp.sum(after * next_state[:, lanes].astype(F32), 0, keepdims=True)
        ending += gather_heads(jnp.broadcast_to(closing, (8, LANES)), expand)
        next_state[:, lanes] = before_low
        reached = (d_y * reach[:, cut]).astype(BF16)
        d_queries += dot(reached, before_low, NT)
        d_keys += dot((scaled * tail[:, cut]).astype(BF16), after_low, NT)
        adjoint[:, lanes] = decay[:, cut] * after + dot(queries, reached, TN)

        d_conv = d_act * (soft + conv * soft * (1.0 - soft))
        later_x[0:CHUNK, lanes] = d_conv
        back = conv_x[CONV - 1 : CONV, lanes] * d_conv
        for tap in range(CONV - 1):
            back = back + conv_x[tap : tap + 1, lanes] * later_x[pl.ds(CONV - 1 - tap, CHUNK), lanes]
        d_x_raw[:, lanes] = back.astype(BF16)
        for tap in range(CONV):
            conv_x_grad[tap : tap + 1, lanes] += jnp.sum(
                padded_x[pl.ds(5 + tap, CHUNK), lanes] * d_conv, 0, keepdims=True
            )
        conv_x_grad[CONV : CONV + 1, lanes] += jnp.sum(d_conv, 0, keepdims=True)

    d_scores[0] = jnp.where(keep, d_scores[0], 0.0)
    d_scores[2] = jnp.where(keep, d_scores[2], 0.0)
    corner, beside, end = (d_scores[block].astype(BF16) for block in range(3))
    d_keys += jnp.concatenate(
        [dot(jnp.concatenate([corner, beside], 1), queries), dot(end, queries[HALF:])], 0
    )
    d_queries += jnp.concatenate(
        [
            dot(corner, keys[0:HALF], TN),
            dot(jnp.concatenate([beside, end], 0), keys, TN),
        ],
        0,
    )
    for index, lanes in enumerate(slabs(2 * STATE)):
        conv = convolve(padded_bc, conv_bc, bias_bc, lanes)
        soft = sigmoid(conv)
        d_conv = (d_keys, d_queries)[index] * (soft + conv * soft * (1.0 - soft))
        later_bc[0:CHUNK, lanes] = d_conv
        back = conv_bc[CONV - 1 : CONV, lanes] * d_conv
        for tap in range(CONV - 1):
            back = back + conv_bc[tap : tap + 1, lanes] * later_bc[pl.ds(CONV - 1 - tap, CHUNK), lanes]
        d_bc_raw[:, lanes] = back.astype(BF16)
        for tap in range(CONV):
            conv_bc_grad[tap : tap + 1, lanes] += jnp.sum(
                padded_bc[pl.ds(5 + tap, CHUNK), lanes] * d_conv, 0, keepdims=True
            )
        conv_bc_grad[CONV : CONV + 1, lanes] += jnp.sum(d_conv, 0, keepdims=True)

    d_cumul = d_mix_sum - skip_heads[...] * d_skip_sum - steps * d_steps
    d_decay = (
        dot(triangle(CHUNK, False).astype(F32), d_cumul, precision=lax.Precision.HIGHEST) + ending[0:1]
    )
    pre = dt_raw[...].astype(F32) + dt_bias[...]
    d_pre = (d_steps + rate[...] * d_decay) * sigmoid(pre)
    d_dt_raw[...] = d_pre.astype(BF16)
    head_grads[0:1] += jnp.sum(d_pre, 0, keepdims=True)
    head_grads[1:2] += jnp.sum(d_decay * steps * rate[...], 0, keepdims=True)
    head_grads[2:3] += jnp.sum(d_skip_sum, 0, keepdims=True)

    @pl.when(step == steps_here - 1)
    def _():
        first_x[...] = later_x[0:8]
        first_bc[...] = later_bc[0:8]


def shape(extent, dtype):
    return jax.ShapeDtypeStruct(extent, dtype)


def whole(array):
    rank = array.ndim if hasattr(array, "ndim") else len(array.shape)
    return pl.BlockSpec(array.shape, lambda step: (0,) * rank)


def params():
    return pltpu.CompilerParams(
        dimension_semantics=("arbitrary",), vmem_limit_bytes=VMEM_LIMIT
    )


def cost(flops, moved):
    return pl.CostEstimate(flops=int(flops), bytes_accessed=int(moved), transcendentals=0)


def by_chunk(width, turn, block=0):
    return pl.BlockSpec((CHUNK, width), lambda step: (turn(step), block))


def from_behind(value, axis, by):
    size = lax.axis_size(axis)
    pairs = [(i, i + by) for i in range(size) if 0 <= i + by < size]
    return lax.ppermute(value, axis, pairs)


def transposed_times(left, right):
    return dot(left, right, TN)


def per_device(
    hidden_in,
    norm_gain,
    w_z,
    w_x,
    w_bc,
    w_dt,
    conv_x,
    conv_x_bias,
    conv_bc,
    conv_bc_bias,
    dt_bias,
    a_log,
    d_skip,
    gate_gain,
    w_out,
    out_grad,
):
    tokens, width = hidden_in.shape
    own_rows = out_grad.shape[0]
    heads_here = w_dt.shape[1]
    inner = w_z.shape[1]
    states_here = w_bc.shape[2]
    chunks = tokens // CHUNK
    ahead = lambda step: step
    behind = lambda step: chunks - 1 - step
    seq_size = lax.axis_size("seq")
    seq_index = lax.axis_index("seq")
    first_row = lax.axis_index("head") * own_rows

    def lane_row(vector):
        return jnp.pad(vector, (0, LANES - heads_here))[None, :]

    piece = lax.all_gather(out_grad, "head", axis=0, tiled=True)
    w_bc_parts = lax.all_gather(w_bc.reshape(width, 2 * states_here), "head")
    small_parts = lax.all_gather(
        jnp.concatenate([conv_bc, conv_bc_bias[None]], 0).reshape((CONV + 1) * 2, states_here), "head"
    )
    w_bc_all = (
        w_bc_parts.reshape(-1, width, 2, states_here).transpose(1, 2, 0, 3).reshape(width, 2 * STATE)
    )
    small = (
        small_parts.reshape(-1, CONV + 1, 2, states_here).transpose(1, 2, 0, 3).reshape(CONV + 1, 2 * STATE)
    )
    conv_bc_all, bias_bc_all = small[0:CONV], small[CONV:]
    w_dt_wide = jnp.pad(w_dt, ((0, 0), (0, LANES - heads_here)))
    dt_bias_row = lane_row(dt_bias)
    rate = lane_row(-jnp.exp(a_log))
    skip_heads = lane_row(d_skip)
    skip = jnp.repeat(d_skip, HEAD_DIM)[None, :]
    gain = gate_gain[None, :]
    bias_x = conv_x_bias[None, :]
    expander = (
        lax.broadcasted_iota(jnp.int32, (LANES, inner), 0)
        == lax.broadcasted_iota(jnp.int32, (LANES, inner), 1) // HEAD_DIM
    ).astype(BF16)

    hidden_f = hidden_in.astype(F32)
    normed_in = (
        hidden_f * lax.rsqrt(jnp.mean(hidden_f * hidden_f, -1, keepdims=True) + EPSILON) * norm_gain
    ).astype(BF16)
    proj_x = dot(normed_in, w_x).astype(BF16)
    proj_bc = dot(normed_in, w_bc_all).astype(BF16)
    proj_dt = dot(normed_in, w_dt_wide).astype(BF16)
    edge_x, edge_bc = from_behind((proj_x[-8:], proj_bc[-8:]), "seq", 1)
    proj_z = dot(normed_in, w_z).astype(BF16)

    wide = by_chunk(inner, ahead)
    lanes_f = by_chunk(LANES, ahead)
    pair_spec = by_chunk(2 * STATE, ahead)
    x_act, bc_act, steps, cumul, packed = pl.pallas_call(
        local_state_kernel,
        grid=(chunks,),
        in_specs=[wide, pair_spec, lanes_f]
        + [whole(a) for a in (edge_x, edge_bc, conv_x, bias_x, conv_bc_all, bias_bc_all)]
        + [whole(a) for a in (dt_bias_row, rate, expander)],
        out_specs=[
            wide, pair_spec, lanes_f, lanes_f,
            pl.BlockSpec((STATE + 16, inner), lambda step: (0, 0)),
        ],
        out_shape=[
            shape((tokens, inner), BF16),
            shape((tokens, 2 * STATE), BF16),
            shape((tokens, LANES), F32),
            shape((tokens, LANES), F32),
            shape((STATE + 16, inner), BF16),
        ],
        scratch_shapes=[
            pltpu.VMEM((CHUNK + 8, inner), F32),
            pltpu.VMEM((CHUNK + 8, 2 * STATE), F32),
            pltpu.VMEM((STATE, inner), F32),
            pltpu.VMEM((1, LANES), F32),
        ],
        compiler_params=params(),
        cost_estimate=cost(1.5e9, 20e6),
        name="local_state",
    )(
        proj_x, proj_bc, proj_dt, edge_x, edge_bc, conv_x, bias_x, conv_bc_all, bias_bc_all,
        dt_bias_row, rate, expander,
    )

    gathered = lax.all_gather(packed, "seq")
    d_normed = dot(piece, w_out, NT).astype(BF16)
    totals = gathered[:, STATE].astype(F32) + gathered[:, STATE + 1].astype(F32)
    place = jnp.arange(seq_size)
    between = (place[None, :] > place[:, None]) & (place[None, :] < seq_index)
    since = jnp.sum(jnp.where(between[:, :, None], totals[None], 0.0), 1)
    weight_in = jnp.where((place < seq_index)[:, None], jnp.exp(since), 0.0)
    state_in = jnp.sum(weight_in[:, None, :] * gathered[:, 0:STATE].astype(F32), 0)
    until = (place[None, :] < place[:, None]) & (place[None, :] > seq_index)
    ahead_of = jnp.sum(jnp.where(until[:, :, None], totals[None], 0.0), 1)
    weight_back = jnp.where((place > seq_index)[:, None], jnp.exp(ahead_of), 0.0)
    final_state = (jnp.exp(totals[seq_index])[None] * state_in + packed[0:STATE].astype(F32)).astype(BF16)

    mixed, sums, states = pl.pallas_call(
        forward_kernel,
        grid=(chunks,),
        in_specs=[wide, pair_spec, lanes_f, lanes_f, wide, wide]
        + [whole(a) for a in (state_in, skip, gain, expander)],
        out_specs=[wide, lanes_f, pl.BlockSpec((1, STATE, inner), lambda step: (step, 0, 0))],
        out_shape=[
            shape((tokens, inner), BF16),
            shape((tokens, LANES), F32),
            shape((chunks, STATE, inner), BF16),
        ],
        scratch_shapes=[
            pltpu.VMEM((STATE, inner), F32),
            pltpu.VMEM((3, HALF, HALF), F32),
            pltpu.VMEM((CHUNK, 2 * CHUNK), BF16),
            pltpu.VMEM((CHUNK, LANES), F32),
            pltpu.VMEM((CHUNK, LANES), F32),
        ],
        compiler_params=params(),
        cost_estimate=cost(10e9, 20e6),
        name="forward_scan",
    )(x_act, bc_act, steps, cumul, proj_z, d_normed, state_in, skip, gain, expander)

    sums = lax.psum(sums[:, 0:2], "head")

    wide_r = by_chunk(inner, behind)
    lanes_r = by_chunk(LANES, behind)
    pair_r = by_chunk(2 * STATE, behind)
    normed_out, d_mixed, grad_z, gain_grad, adjoint_packed = pl.pallas_call(
        gate_kernel,
        grid=(chunks,),
        in_specs=[wide_r, wide_r, wide_r, by_chunk(2, behind), pair_r, lanes_r]
        + [whole(a) for a in (gain, expander)],
        out_specs=[
            wide_r, wide_r, wide_r,
            pl.BlockSpec((8, inner), lambda step: (0, 0)),
            pl.BlockSpec((STATE, inner), lambda step: (0, 0)),
        ],
        out_shape=[
            shape((tokens, inner), BF16),
            shape((tokens, inner), BF16),
            shape((tokens, inner), BF16),
            shape((8, inner), F32),
            shape((STATE, inner), BF16),
        ],
        scratch_shapes=[pltpu.VMEM((STATE, inner), F32), pltpu.VMEM((8, inner), F32)],
        compiler_params=params(),
        cost_estimate=cost(1.5e9, 20e6),
        name="gate",
    )(mixed, proj_z, d_normed, sums, bc_act, cumul, gain, expander)

    adjoints = lax.all_gather(adjoint_packed, "seq")
    w_out_grad = dot(normed_out, piece, TN)
    w_z_grad = dot(normed_in, grad_z, TN)
    w_out_sum = lax.psum(w_out_grad.astype(BF16), "seq")
    w_z_sum = lax.psum(w_z_grad.astype(BF16), "seq")
    out_part = lax.psum_scatter(
        dot(normed_out, w_out).astype(BF16), "head", scatter_dimension=0, tiled=True
    )
    hidden_own = lax.dynamic_slice_in_dim(hidden_in, first_row, own_rows, 0).astype(F32)
    output = (hidden_own + out_part.astype(F32)).astype(BF16)
    adjoint_in = jnp.sum(weight_back[:, None, :] * adjoints.astype(F32), 0)

    def rows_before(width_here, block=0):
        per = CHUNK // 16
        return pl.BlockSpec(
            (16, width_here), lambda step: (jnp.maximum(behind(step) * per - 1, 0), block)
        )

    constants = (conv_x, bias_x, conv_bc_all, bias_bc_all, dt_bias_row, rate, skip, skip_heads, expander)
    grad_x, grad_bc, grad_dt, first_x, first_bc, conv_x_sums, conv_bc_sums, head_sums = pl.pallas_call(
        backward_kernel,
        grid=(chunks,),
        in_specs=[
            wide_r, rows_before(inner), pair_r, rows_before(2 * STATE), lanes_r,
            whole(edge_x), whole(edge_bc), pair_r, lanes_r, lanes_r, wide_r, wide_r,
            pl.BlockSpec((1, STATE, inner), lambda step: (behind(step), 0, 0)),
            whole(final_state), whole(adjoint_in),
        ]
        + [whole(a) for a in constants],
        out_specs=[wide_r, pair_r, lanes_r]
        + [
            pl.BlockSpec((8, width_here), lambda step: (0, 0))
            for width_here in (inner, 2 * STATE, inner, 2 * STATE, LANES)
        ],
        out_shape=[
            shape((tokens, inner), BF16),
            shape((tokens, 2 * STATE), BF16),
            shape((tokens, LANES), BF16),
        ]
        + [shape((8, width_here), F32) for width_here in (inner, 2 * STATE, inner, 2 * STATE, LANES)],
        scratch_shapes=[
            pltpu.VMEM((CHUNK + 8, inner), F32),
            pltpu.VMEM((CHUNK + 8, 2 * STATE), F32),
            pltpu.VMEM((CHUNK + 8, inner), F32),
            pltpu.VMEM((CHUNK + 8, 2 * STATE), F32),
            pltpu.VMEM((STATE, inner), F32),
            pltpu.VMEM((STATE, inner), BF16),
            pltpu.VMEM((3, HALF, HALF), F32),
            pltpu.VMEM((CHUNK, 2 * CHUNK), BF16),
            pltpu.VMEM((3, HALF, HALF), F32),
            pltpu.VMEM((CHUNK, LANES), F32),
            pltpu.VMEM((CHUNK, LANES), F32),
        ],
        compiler_params=params(),
        cost_estimate=cost(25e9, 25e6),
        name="backward_scan",
    )(
        proj_x, proj_x, proj_bc, proj_bc, proj_dt, edge_x, edge_bc, bc_act, steps, cumul, mixed, d_mixed,
        states, final_state, adjoint_in, *constants,
    )

    next_x, next_bc = from_behind((first_x, first_bc), "seq", -1)

    def close_edge(grad, taps, following):
        rows = []
        for row in range(CONV - 1):
            rows.append(
                sum(
                    taps[tap] * following[row + CONV - 1 - tap - (CONV - 1)]
                    for tap in range(CONV - 1)
                    if row + CONV - 1 - tap - (CONV - 1) >= 0
                )
            )
        extra = jnp.concatenate([jnp.zeros((16 - (CONV - 1), grad.shape[1]), F32), jnp.stack(rows)], 0)
        ending = (grad[-16:].astype(F32) + extra).astype(BF16)
        return lax.dynamic_update_slice(grad, ending, (tokens - 16, 0))

    grad_x = close_edge(grad_x, conv_x, next_x)
    grad_bc = close_edge(grad_bc, conv_bc_all, next_bc)

    w_x_grad = dot(normed_in, grad_x, TN)
    w_bc_grad = dot(normed_in, grad_bc, TN)
    w_dt_grad = dot(normed_in, grad_dt, TN)[:, 0:heads_here]
    d_rows = dot(grad_z, w_z, NT) + dot(grad_x, w_x, NT)
    d_rows = d_rows + dot(grad_bc, w_bc_all, NT) + dot(grad_dt, w_dt_wide, NT)
    d_normed_rows = lax.psum_scatter(
        d_rows.astype(BF16), "head", scatter_dimension=0, tiled=True
    ).astype(F32)
    w_x_sum = lax.psum(w_x_grad.astype(BF16), "seq")

    def own_states(partial):
        rows = partial.shape[0]
        parts = partial.reshape(rows, 2, -1, states_here).transpose(2, 0, 1, 3)
        return lax.psum_scatter(parts, "head", scatter_dimension=0, tiled=False)

    w_bc_own = own_states(w_bc_grad.astype(BF16))
    conv_bc_own = own_states(conv_bc_sums[0 : CONV + 1])

    inverse = lax.rsqrt(jnp.mean(hidden_own * hidden_own, -1, keepdims=True) + EPSILON)
    weighted = d_normed_rows * norm_gain
    dots = jnp.sum(weighted * hidden_own, -1, keepdims=True)
    input_grad = (
        out_grad.astype(F32)
        + inverse * weighted
        - hidden_own * (inverse * inverse * inverse * dots / width)
    )
    gain_part = jnp.sum(d_normed_rows * hidden_own * inverse, 0)
    norm_gain_grad = lax.psum(gain_part, ("seq", "head"))
    w_bc_sum, w_dt_sum = lax.psum((w_bc_own, w_dt_grad.astype(BF16)), "seq")
    conv_x_all, conv_bc_sum, head_all, gate_gain_grad = lax.psum(
        (conv_x_sums[0 : CONV + 1], conv_bc_own, head_sums[0:3, 0:heads_here], gain_grad[0]), "seq"
    )
    return (
        output,
        input_grad,
        norm_gain_grad,
        w_z_sum.astype(F32),
        w_x_sum.astype(F32),
        w_bc_sum.astype(F32),
        w_dt_sum.astype(F32),
        conv_x_all[0:CONV],
        conv_x_all[CONV],
        conv_bc_sum[0:CONV],
        conv_bc_sum[CONV],
        head_all[0],
        head_all[1],
        head_all[2],
        gate_gain_grad,
        w_out_sum.astype(F32),
    )


def solution(mesh):
    placed = (
        P("seq", None),
        P(),
        P(None, "head"),
        P(None, "head"),
        P(None, None, "head"),
        P(None, "head"),
        P(None, "head"),
        P("head"),
        P(None, None, "head"),
        P(None, "head"),
        P("head"),
        P("head"),
        P("head"),
        P("head"),
        P("head", None),
        P(("seq", "head"), None),
    )
    return jax.shard_map(
        per_device,
        mesh=mesh,
        in_specs=placed,
        out_specs=(
            P(("seq", "head"), None),
            P(("seq", "head"), None),
            P(),
            P(None, "head"),
            P(None, "head"),
            P(None, None, "head"),
            P(None, "head"),
            P(None, "head"),
            P("head"),
            P(None, None, "head"),
            P(None, "head"),
            P("head"),
            P("head"),
            P("head"),
            P("head"),
            P("head", None),
        ),
        check_vma=False,
    )
```

time: 2180 us -> 779 us (0.36)
  local copies, waits for them, and re-layouts: 662 us -> 14.3 us
  matrix products: 464 us -> 117 us
  waiting for transfers between devices: 612 us -> 291 us
  other arithmetic: 308 us -> 41.8 us
  Pallas kernels: 0 us -> 112 us
  blocking collectives: 77.2 us -> 167 us
    psum x1, waiting for transfers between devices: 456 us -> 101 us  [per_device(): w_z_sum = lax.psum(w_z_grad.astype(BF16), 'seq')]
    dot_general x128 -> x15, matrix products: 460 us -> 117 us  [dot(): lax.dot_general(left, right, (contract, ((), ())), preferred_element_type...]
    dynamic_update_slice x56 -> x0, local copies, waits for them, and re-layouts: 341 us -> none  [block_scan(): final, results = lax.scan(jax.checkpoint(advance), state, pieces)]
    another operation x113 -> x0, other arithmetic: 130 us -> none
    pallas_call x0 -> x4, Pallas kernels: none -> 112 us  [the longest x1 57.5 us: per_device(): pl.pallas_call(backward_kernel, grid=(chunks,), in_specs=[wide_r, rows_be...]
    another operation x129 -> x2, local copies, waits for them, and re-layouts: 86.6 us -> 0.68 us  [the longest x1 0.67 us: per_device(): skip = jnp.repeat(d_skip, HEAD_DIM)[None, :]]
    psum x4, blocking collectives: 56.7 us -> 141 us  [the longest x1 39.9 us: per_device(): lax.psum((conv_x_sums[0:CONV + 1], conv_bc_own, head_sums[0:3, 0:heads_he...]
    reduce_sum x27 -> x6, other arithmetic: 76.2 us -> 15 us  [the longest x1 4.23 us: per_device(): jnp.mean(hidden_f * hidden_f, -1, keepdims=True) + EPSILON]
  transfers between devices with their start and end apart: 12 -> 11, of which waited for: 7 -> 7; matrix products, arithmetic and copies ran while one was open for 23% -> 19% of each run, Pallas kernels for 0% -> 0%
where the time goes in v1:
time: 779 us; the launch traced here: 770 us
  waiting for transfers between devices  291 us (37%)
  blocking collectives  167 us (21%)
  matrix products  117 us (15%)
  Pallas kernels  112 us (14%)
  other arithmetic  41.8 us (5%)
  between operations  15.2 us (2%)
  local copies, waits for them, and re-layouts  14.3 us (2%)
  starting transfers between devices  10.9 us (1%)
    dot_general x15, matrix products, dot(): lax.dot_general(left, right, (contract, ((), ())), preferred_element_type...  117 us
    psum x1, waiting for transfers between devices, per_device(): w_z_sum = lax.psum(w_z_grad.astype(BF16), 'seq')  101 us
    pallas_call x1, Pallas kernels, per_device(): pl.pallas_call(backward_kernel, grid=(chunks,), in_specs=[wide_r, rows_be...  57.5 us
    reduce_scatter x1, waiting for transfers between devices, per_device(): lax.psum_scatter(d_rows.astype(BF16), 'head', scatter_dimension=0, tiled=...  47.2 us
    all_gather x1, waiting for transfers between devices, per_device(): piece = lax.all_gather(out_grad, 'head', axis=0, tiled=True)  42.1 us
    psum x1, blocking collectives, per_device(): lax.psum((conv_x_sums[0:CONV + 1], conv_bc_own, head_sums[0:3, 0:heads_he...  39.9 us
    psum x1, blocking collectives, per_device(): norm_gain_grad = lax.psum(gain_part, ('seq', 'head'))  39.7 us
    psum x1, blocking collectives, per_device(): w_bc_sum, w_dt_sum = lax.psum((w_bc_own, w_dt_grad.astype(BF16)), 'seq')  34.4 us
  transfers between devices with their start and end apart: 11, of which 7 were waited for; matrix products, arithmetic and copies ran while one was open for 19% of the time, Pallas kernels for 0%

profile of v1, /device:TPU:0, one launch (start us, length us, event | category | flops | bytes accessed | tf_op | source)
XLA Modules:
  0.0 769.8 jit_solution(569217980555752146)
XLA Ops:
  7.3 4.2 fusion
  11.5 10.2 %all_gather.21 = bf16[4,1536,64]{1,2,0:T(8,128)(2,1)S(1)} all-gather(bf16[1,1536,64]{1,2,0:T(8,128)(2,1)S(1)} %bitcast.80), channel_id=1, replica_groups=mesh['seq'=8,'head'=4] {'head'}, dimensions={0}, use_global_device_ids=true | all-gather | bytes 983040 | tf_op jit(solution)/shard_map/all_gather | solution.py:472
  21.8 1.5 fusion.2
  23.3 1.9 convolution_convert_fusion.8.bc_raw.bc_before
  25.3 3.6 collective-permute-start.1
  28.9 5.2 convolution_convert_fusion.6.x_raw.x_before
  34.2 3.4 collective-permute-start
  37.7 5.2 all_gather.22
  43.0 5.3 convolution_convert_fusion.9.dt_raw
  52.1 22.2 %local_state.1 = (bf16[2048,768]{1,0:T(8,128)(2,1)}, bf16[2048,256]{1,0:T(8,128)(2,1)}, f32[2048,128]{1,0:T(8,128)}, f32[2048,128]{1,0:T(8,128)}, bf16[144,768]{1,0:T(8,128)(2,1)}) custom-call(bf16[2048,768]{1,0:T(8,128)(2,1)} %copy-done.29, bf16[2048,256]{1,0:T(8,128)(2,1)} %copy-done.30, bf16[2048,128]{1,0:T(8,128)(2,1)} %convolution_convert_fusion.9.dt_raw, ...), custom_call_target="tpu_custom_call" | custom-call | flops 1500000000 | bytes 20000000 | tf_op jit(solution)/shard_map/local_state/pallas_call | solution.py:508
  77.0 9.2 %convolution_convert_fusion.5.gate = bf16[2048,768]{1,0:T(8,128)(2,1)} fusion(bf16[2048,1536]{1,0:T(8,128)(2,1)} %copy-done.2, bf16[1536,768]{1,0:T(8,128)(2,1)S(1)} %copy-done), kind=kOutput, calls=%fused_computation.18 | convolution fusion | flops 4833411072 | bytes 11796480 | tf_op jit(solution)/shard_map/dot_general | solution.py:24
  86.2 34.1 %all-gather.8.cloned.1.call-done = bf16[1152,768]{1,0:T(8,128)(2,1)} async-done(((bf16[144,768]{1,0:T(8,128)(2,1)}), bf16[1152,768]{1,0:T(8,128)(2,1)}) %all-gather.8.cloned.1.call-update) | async-done | bytes 1769488 | tf_op jit(solution)/shard_map/all_gather | solution.py:539
  122.7 2.5 multiply_reduce_fusion.state_in
  125.2 42.1 %all-gather.6.cloned.1.call-done = bf16[2048,1536]{1,0:T(8,128)(2,1)} async-done(((bf16[512,1536]{1,0:T(8,128)(2,1)}), bf16[2048,1536]{1,0:T(8,128)(2,1)}) %all-gather.6.cloned.1.call-update) | async-done | bytes 6291472 | tf_op jit(solution)/shard_map/all_gather | solution.py:471
  167.3 9.0 %convolution_convert_fusion.4.d_normed = bf16[2048,768]{1,0:T(8,128)(2,1)} fusion(bf16[2048,1536]{1,0:T(8,128)(2,1)} %all-gather.6.cloned.1.call-done, bf16[768,1536]{1,0:T(8,128)(2,1)} %param.30), kind=kOutput, calls=%fused_computation.17 | convolution fusion | flops 4833411072 | bytes 11796480 | tf_op jit(solution)/shard_map/dot_general | solution.py:24
  176.3 18.2 %forward_scan.1 = (bf16[2048,768]{1,0:T(8,128)(2,1)}, f32[2048,128]{1,0:T(8,128)}, bf16[8,128,768]{2,1,0:T(8,128)(2,1)}) custom-call(bf16[2048,768]{1,0:T(8,128)(2,1)} %get-tuple-element.37.x_act, bf16[2048,256]{1,0:T(8,128)(2,1)} %get-tuple-element.38.bc_act, f32[2048,128]{1,0:T(8,128)} %get-tuple-element.39.dt_in, f32[2048,128]{1,0:T(8,128)} %get-tuple-element.40.cumul_in, ...), custom_call_target="tpu_custom_call" | custom-call | flops 10000000000 | bytes 20000000 | tf_op jit(solution)/shard_map/forward_scan/pallas_call | solution.py:552
  194.6 26.6 %psum.77.sums = f32[2048,2]{1,0:T(8,128)} all-reduce(f32[2048,2]{1,0:T(8,128)} %bitcast.78), channel_id=1, replica_groups=mesh['seq'=8,'head'=4] {'head'}, use_global_device_ids=true, to_apply=%region_3.4 | all-reduce | flops 4096 | bytes 32768 | tf_op jit(solution)/shard_map/psum | solution.py:575
  221.2 14.3 %gate.1 = (bf16[2048,768]{1,0:T(8,128)(2,1)}, bf16[2048,768]{1,0:T(8,128)(2,1)}, bf16[2048,768]{1,0:T(8,128)(2,1)}, f32[8,768]{1,0:T(8,128)}, bf16[128,768]{1,0:T(8,128)(2,1)}) custom-call(bf16[2048,768]{1,0:T(8,128)(2,1)} %get-tuple-element.42.mixed_in, bf16[2048,768]{1,0:T(8,128)(2,1)} %convolution_convert_fusion.5.gate, ...), custom_call_target="tpu_custom_call" | custom-call | flops 1500000000 | bytes 20000000 | tf_op jit(solution)/shard_map/gate/pallas_call | solution.py:580
  239.2 1.6 add_convert_fusion.1.final_state
  240.9 9.2 %convolution_convert_fusion.3 = bf16[1536,768]{1,0:T(8,128)(2,1)} fusion(bf16[2048,1536]{1,0:T(8,128)(2,1)} %copy-done.2, bf16[2048,768]{1,0:T(8,128)(2,1)} %get-tuple-element.45), kind=kOutput, calls=%fused_computation.16 | convolution fusion | flops 4833017856 | bytes 11796480 | tf_op jit(solution)/shard_map/dot_general | solution.py:24
  250.1 30.9 %all-gather.10.cloned.1.call-done = bf16[1024,768]{1,0:T(8,128)(2,1)} async-done(((bf16[128,768]{1,0:T(8,128)(2,1)}), bf16[1024,768]{1,0:T(8,128)(2,1)}) %all-gather.10.cloned.1.call-update) | async-done | bytes 1572880 | tf_op jit(solution)/shard_map/all_gather | solution.py:603
  281.0 2.5 fusion.11.adjoint_in
  283.5 57.5 %backward_scan.1 = (bf16[2048,768]{1,0:T(8,128)(2,1)}, bf16[2048,256]{1,0:T(8,128)(2,1)}, bf16[2048,128]{1,0:T(8,128)(2,1)}, f32[8,768]{1,0:T(8,128)}, f32[8,256...) custom-call(bf16[2048,768]{1,0:T(8,128)(2,1)} %copy-done.29, bf16[2048,768]{1,0:T(8,128)(2,1)} %copy-done.29, ...), custom_call_target="tpu_custom_call" | custom-call | flops 24999999488 | bytes 25000000 | tf_op jit(solution)/shard_map/backward_scan/pallas_call | solution.py:622
  342.3 9.2 %convolution_convert_fusion.1 = bf16[768,1536]{1,0:T(8,128)(2,1)} fusion(bf16[2048,768]{1,0:T(8,128)(2,1)S(1)} %copy-done.31, bf16[2048,1536]{1,0:T(8,128)(2,1)} %all-gather.6.cloned.1.call-done), kind=kOutput, calls=%fused_computation.14 | convolution fusion | flops 4833017856 | bytes 11796480 | tf_op jit(solution)/shard_map/dot_general | solution.py:24
  351.5 1.5 collective-permute-start.2
  353.1 5.0 convolution_convert_fusion.7
  360.7 9.2 %convolution_convert_fusion.2 = bf16[1536,768]{1,0:T(8,128)(2,1)} fusion(bf16[2048,1536]{1,0:T(8,128)(2,1)} %copy-done.2, bf16[2048,768]{1,0:T(8,128)(2,1)} %fusion.19), kind=kOutput, calls=%fused_computation.15 | convolution fusion | flops 4833017856 | bytes 11796480 | tf_op jit(solution)/shard_map/dot_general | solution.py:24
  369.9 15.6 %reduce-scatter.8.cloned.1.call-done = bf16[1,1536,2,32]{1,3,2,0:T(8,128)(2,1)} async-done(((bf16[4,1536,2,32]{1,3,2,0:T(8,128)(2,1)}), bf16[1,1536,2,32]{1,3,2,0:T(8,128)(2,1)}) %reduce-scatter.8.cloned.1.call-update) | async-done | bytes 196624 | tf_op jit(solution)/shard_map/reduce_scatter | solution.py:696
  385.6 10.1 %fusion.37 = f32[2048,1536]{1,0:T(8,128)} fusion(bf16[2048,768]{1,0:T(8,128)(2,1)} %get-tuple-element.45, bf16[1536,768]{1,0:T(8,128)(2,1)S(1)} %copy-done), kind=kOutput, calls=%fused_computation.100 | convolution fusion | flops 4831838208 | bytes 18087936 | tf_op jit(solution)/shard_map/dot_general | solution.py:24
  395.7 6.7 fusion.39
  402.4 8.3 %fusion.38 = f32[2048,1536]{1,0:T(8,128)} fusion(bf16[2048,768]{1,0:T(8,128)(2,1)S(1)} %copy-done.28, bf16[1536,768]{1,0:T(8,128)(2,1)S(1)} %copy-done.33), kind=kOutput, calls=%fused_computation.101 | convolution fusion | flops 4831838208 | bytes 18087936 | tf_op jit(solution)/shard_map/dot_general | solution.py:24
  410.7 15.9 %add_convert_fusion = bf16[2048,1536]{1,0:T(8,128)(2,1)} fusion(f32[2048,1536]{1,0:T(8,128)} %fusion.39, f32[2048,1536]{1,0:T(8,128)} %fusion.37, f32[2048,1536]{1,0:T(8,128)} %fusion.38, bf16[2048,128]{1,0:T(8,128)(2,1)S(1)} %copy-done.9, bf16[1536,12]{0,1:T(8,128)(2,1)S(1)} %copy-done.16), kind=kOutput, calls=%fused_computation.5 | convolution fusion | flops 817889280 | bytes 44601344 | tf_op jit(solution)/shard_map/dot_general | solution.py:24
  426.9 9.1 %convolution_convert_fusion = bf16[2048,1536]{1,0:T(8,128)(2,1)} fusion(bf16[2048,768]{1,0:T(8,128)(2,1)} %get-tuple-element.44, bf16[768,1536]{1,0:T(8,128)(2,1)} %param.30), kind=kOutput, calls=%fused_computation.6 | convolution fusion | flops 4834983936 | bytes 11796480 | tf_op jit(solution)/shard_map/dot_general | solution.py:24
  437.3 1.9 fusion.7
  440.1 11.1 %all-reduce.4 = f32[4,5,2,32]{3,2,1,0:T(2,128)S(1)} all-reduce(f32[4,5,2,32]{3,2,1,0:T(2,128)S(1)} %bitcast.85), channel_id=7, replica_groups=mesh['seq'=8,'head'=4] {'head'}, use_global_device_ids=true, to_apply=%region_18.19.clone | all-reduce | flops 1280 | bytes 10240
  451.8 39.9 %all-reduce.5 = (f32[5,768]{1,0:T(8,128)S(1)}, f32[5,2,32]{2,1,0:T(2,128)S(1)}, f32[3,12]{1,0:T(4,128)S(1)}, f32[768]{0:T(1024)}) all-reduce(f32[5,768]{1,0:T(8,128)S(1)} %bitcast.86, f32[5,2,32]{2,1,0:T(2,128)S(1)} %dynamic-slice_bitcast_fusion, f32[3,12]{1,0:T(4,128)S(1)} %slice.162, ...), channel_id=1, replica_groups=mesh['seq'=8,'head'=4] {'seq'}, use_global_device_ids=true, to_apply=%region_17.18 | all-reduce | flops 4964 | bytes 39712 | tf_op jit(solution)/shard_map/psum | solution.py:712
  492.9 3.8 fusion.40
  496.8 34.4 %psum.82 = bf16[1536,12]{0,1:T(8,128)(2,1)S(1)} all-reduce(bf16[1536,12]{0,1:T(8,128)(2,1)S(1)} %slice.231), channel_id=1, replica_groups=mesh['seq'=8,'head'=4] {'seq'}, use_global_device_ids=true, to_apply=%region_16.17 | all-reduce | flops 18432 | bytes 73728 | tf_op jit(solution)/shard_map/psum | solution.py:711
  533.5 101.2 %all-reduce.9.cloned.1.call-done = (bf16[1536,768]{1,0:T(8,128)(2,1)}, bf16[1536,768]{1,0:T(8,128)(2,1)}, bf16[1536,2,32]{0,2,1:T(8,128)(2,1)}, bf16[768,1536]{1,0:T(8,128)(2,1)}) async-done(((bf16[1536,768]{1,0:T(8,128)(2,1)}, bf16[1536,768]{1,0:T(8,128)(2,1)}, bf16[1536,2,32]{0,2,1:T(8,128)(2,1)}, bf16[768,1536]{1,0:T(8,128)(2,1)}), (bf16[1536,768]{1,0:T(8,128)(2,1)}, bf16[1536,768]{1,0:T(8,128)(2,1)}, ...) | async-done | bytes 7274512 | tf_op jit(solution)/shard_map/psum | solution.py:607
  634.8 1.7 convert_element_type.155
  636.5 4.4 convert_element_type.151
  640.8 2.8 convert_element_type.153
  644.1 3.2 convert_element_type.158
  647.3 47.2 %reduce-scatter.6.cloned.1.call-done = bf16[512,1536]{1,0:T(8,128)(2,1)} async-done(((bf16[2048,1536]{1,0:T(8,128)(2,1)}), bf16[512,1536]{1,0:T(8,128)(2,1)}) %reduce-scatter.6.cloned.1.call-update) | async-done | bytes 1572880 | tf_op jit(solution)/shard_map/reduce_scatter | solution.py:688
  694.5 3.1 fusion.10
  697.6 39.7 %psum.78 = f32[1536]{0:T(1024)} all-reduce(f32[1536]{0:T(1024)S(1)} %get-tuple-element.58), channel_id=1, replica_groups=mesh['seq'=8,'head'=4] {'seq','head'}, use_global_device_ids=true, to_apply=%region_11.12 | all-reduce | flops 1536 | bytes 12288 | tf_op jit(solution)/shard_map/psum | solution.py:710
  737.3 19.1 %reduce-scatter.4.cloned.1.call-done = bf16[512,1536]{1,0:T(8,128)(2,1)} async-done(((bf16[2048,1536]{1,0:T(8,128)(2,1)}), bf16[512,1536]{1,0:T(8,128)(2,1)}) %reduce-scatter.4.cloned.1.call-update) | async-done | bytes 1572880 | tf_op jit(solution)/shard_map/reduce_scatter | solution.py:608
  756.4 6.1 fusion.5
  (152 shorter events, 23.8 us)
Async XLA Ops:
  7.2 69.8 %copy-start = (bf16[1536,768]{1,0:T(8,128)(2,1)S(1)}, bf16[1536,768]{1,0:T(8,128)(2,1)}, u32[]{:S(2)}) copy-start(bf16[1536,768]{1,0:T(8,128)(2,1)} %param.18) | copy-start | bytes 7077892
  7.2 4.3 copy-start.10
  7.2 14.6 %copy-start.13 = (f32[1536]{0:T(1024)S(1)}, f32[1536]{0:T(1024)}, u32[]{:S(2)}) copy-start(f32[1536]{0:T(1024)} %param.17) | copy-start | bytes 18436
  7.2 113.1 %all-gather.8.cloned.1.call-start = ((), (), s32[]{:S(2)}) async-start(), calls=%async_computation.7 | async-start | bytes 1990656 | tf_op jit(solution)/shard_map/all_gather | solution.py:539
  7.3 14.5 %copy-start.1 = (bf16[2048,1536]{1,0:T(8,128)(2,1)S(1)}, bf16[2048,1536]{1,0:T(8,128)(2,1)}, u32[]{:S(2)}) copy-start(bf16[2048,1536]{1,0:T(8,128)(2,1)} %param.16) | copy-start | bytes 18874372
  23.3 5.6 copy-start.2
  23.3 5.6 copy-start.32
  25.2 8.9 %copy-start.30 = (bf16[2048,256]{1,0:T(8,128)(2,1)}, bf16[2048,256]{1,0:T(8,128)(2,1)S(1)}, u32[]{:S(2)}) copy-start(bf16[2048,256]{1,0:T(8,128)(2,1)S(1)} %convolution_convert_fusion.8.bc_raw.bc_before) | copy-start | bytes 3145732
  25.3 12.4 %copy-start.37 = (f32[12]{0:T(128)S(1)}, f32[12]{0:T(128)}, u32[]{:S(2)}) copy-start(f32[12]{0:T(128)} %param.27) | copy-start | bytes 148
  25.3 12.4 %copy-start.22 = (f32[4,2,32]{2,1,0:T(2,128)S(1)}, f32[4,2,32]{2,1,0:T(2,128)}, u32[]{:S(2)}) copy-start(f32[4,2,32]{2,1,0:T(2,128)} %param.24) | copy-start | bytes 3076
  25.3 12.4 %copy-start.24 = (f32[2,32]{1,0:T(2,128)S(1)}, f32[2,32]{1,0:T(2,128)}, u32[]{:S(2)}) copy-start(f32[2,32]{1,0:T(2,128)} %param.25) | copy-start | bytes 772
  25.3 17.6 %copy-start.15 = (bf16[1536,12]{0,1:T(8,128)(2,1)S(1)}, bf16[1536,12]{0,1:T(8,128)(2,1)}, u32[]{:S(2)}) copy-start(bf16[1536,12]{0,1:T(8,128)(2,1)} %param.21) | copy-start | bytes 110596
  25.3 26.1 %collective-permute-start.1 = (bf16[8,256]{1,0:T(8,128)(2,1)S(1)}, bf16[8,256]{1,0:T(8,128)(2,1)S(1)}, u32[]{:S(2)}, u32[]{:S(2)}) collective-permute-start(bf16[8,256]{1,0:T(8,128)(2,1)S(1)} %slice.168), channel_id=1, source_target_pairs={{0,4},{4,8},{8,12},{12,16},{16,20},{20,24},{24,28},{1,5},{5,9},{9,... | collective-permute-start | bytes 12296 | tf_op jit(solution)/shard_map/ppermute | solution.py:431
  34.1 3.5 copy-start.29
  34.2 17.3 %collective-permute-start = (bf16[8,768]{1,0:T(8,128)(2,1)S(1)}, bf16[8,768]{1,0:T(8,128)(2,1)S(1)}, u32[]{:S(2)}, u32[]{:S(2)}) collective-permute-start(bf16[8,768]{1,0:T(8,128)(2,1)S(1)} %slice.167), channel_id=1, source_target_pairs={{0,4},{4,8},{8,12},{12,16},{16,20},{20,24},{24,28},{1,5},{5,9},{9,... | collective-permute-start | bytes 36872 | tf_op jit(solution)/shard_map/ppermute | solution.py:431
  42.9 6.1 copy-start.27
  42.9 6.6 copy-start.20
  51.5 0.6 copy-start.35
  52.1 23.5 %copy-start.21 = (f32[768]{0:T(1024)S(1)}, f32[768]{0:T(1024)}, u32[]{:S(2)}) copy-start(f32[768]{0:T(1024)} %param.29) | copy-start | bytes 9220
  52.1 24.1 %copy-start.26 = (f32[12]{0:T(128)S(1)}, f32[12]{0:T(128)}, u32[]{:S(2)}) copy-start(f32[12]{0:T(128)} %param.28) | copy-start | bytes 148
  74.3 93.0 %all-gather.6.cloned.1.call-start = ((), (), s32[]{:S(2)}) async-start(), calls=%async_computation.3 | async-start | bytes 7864320 | tf_op jit(solution)/shard_map/all_gather | solution.py:471
  75.1 205.9 %all-gather.10.cloned.1.call-start = ((), (), s32[]{:S(2)}) async-start(), calls=%async_computation.8 | async-start | bytes 1769472 | tf_op jit(solution)/shard_map/all_gather | solution.py:603
  76.9 9.2 %copy-start.23 = (pred[8]{0:T(512)(128)(4,1)}, pred[8]{0:T(512)(128)(4,1)S(1)}, u32[]{:S(2)}) copy-start(pred[8]{0:T(512)(128)(4,1)S(1)} %iota_compare_fusion.2) | copy-start | bytes 28
  221.1 18.1 %copy-start.5 = (f32[128,768]{1,0:T(8,128)S(1)}, f32[128,768]{1,0:T(8,128)}, u32[]{:S(2)}) copy-start(f32[128,768]{1,0:T(8,128)} %multiply_reduce_fusion.state_in) | copy-start | bytes 1179652
  235.5 150.0 %reduce-scatter.8.cloned.1.call-start = ((), (), s32[]{:S(2)}) async-start(), calls=%async_computation.6 | async-start | bytes 983040 | tf_op jit(solution)/shard_map/reduce_scatter | solution.py:696
  240.9 40.1 %copy-start.12 = (f32[8,768]{1,0:T(8,128)S(1)}, f32[8,768]{1,0:T(8,128)}, u32[]{:S(2)}) copy-start(f32[8,768]{1,0:T(8,128)} %exponential_select_fusion) | copy-start | bytes 73732
  283.5 58.8 %copy-start.31 = (bf16[2048,768]{1,0:T(8,128)(2,1)S(1)}, bf16[2048,768]{1,0:T(8,128)(2,1)}, u32[]{:S(2)}) copy-start(bf16[2048,768]{1,0:T(8,128)(2,1)} %get-tuple-element.44) | copy-start | bytes 9437188
  341.0 12.1 %collective-permute-start.3 = (f32[8,256]{1,0:T(8,128)}, f32[8,256]{1,0:T(8,128)S(1)}, u32[]{:S(2)}, u32[]{:S(2)}) collective-permute-start(f32[8,256]{1,0:T(8,128)} %get-tuple-element.52), channel_id=1, source_target_pairs={{4,0},{8,4},{12,8},{16,12},{20,16},{24,20},{28,24},{5,1},{9,5},{13... | collective-permute-start | bytes 24584 | tf_op jit(solution)/shard_map/ppermute | solution.py:431
  342.3 9.2 %copy-start.34 = (f32[8,768]{1,0:T(8,128)S(1)}, f32[8,768]{1,0:T(8,128)}, u32[]{:S(2)}) copy-start(f32[8,768]{1,0:T(8,128)} %get-tuple-element.50) | copy-start | bytes 73732
  342.3 10.8 %copy-start.6 = (bf16[2048,256]{1,0:T(8,128)(2,1)S(1)}, bf16[2048,256]{1,0:T(8,128)(2,1)}, u32[]{:S(2)}) copy-start(bf16[2048,256]{1,0:T(8,128)(2,1)} %get-tuple-element.51) | copy-start | bytes 3145732
  351.5 7.7 collective-permute-start.2
  353.1 5.0 copy-start.7
  353.1 6.1 copy-start.19
  359.1 275.6 %all-reduce.9.cloned.1.call-start = ((), (), s32[]{:S(2)}) async-start(), calls=%async_computation.9 | async-start | bytes 14548992 | tf_op jit(solution)/shard_map/psum | solution.py:607
  385.5 309.0 %reduce-scatter.6.cloned.1.call-start = ((), (), s32[]{:S(2)}) async-start(), calls=%async_computation.5 | async-start | bytes 7864320 | tf_op jit(solution)/shard_map/reduce_scatter | solution.py:688
  385.6 10.1 %copy-start.8 = (bf16[2048,256]{1,0:T(8,128)(2,1)S(1)}, bf16[2048,256]{1,0:T(8,128)(2,1)}, u32[]{:S(2)}) copy-start(bf16[2048,256]{1,0:T(8,128)(2,1)} %copy-done.7) | copy-start | bytes 3145732
  395.7 6.7 copy-start.28
  395.7 6.7 copy-start.33
  402.4 8.3 %copy-start.9 = (bf16[2048,128]{1,0:T(8,128)(2,1)S(1)}, bf16[2048,128]{1,0:T(8,128)(2,1)}, u32[]{:S(2)}) copy-start(bf16[2048,128]{1,0:T(8,128)(2,1)} %get-tuple-element.53) | copy-start | bytes 1572868
  402.4 8.3 %copy-start.16 = (bf16[1536,12]{0,1:T(8,128)(2,1)S(1)}, bf16[1536,12]{0,1:T(8,128)(2,1)}, u32[]{:S(2)}) copy-start(bf16[1536,12]{0,1:T(8,128)(2,1)} %param.21) | copy-start | bytes 110596
  426.6 329.7 %reduce-scatter.4.cloned.1.call-start = ((), (), s32[]{:S(2)}) async-start(), calls=%async_computation.4 | async-start | bytes 7864320 | tf_op jit(solution)/shard_map/reduce_scatter | solution.py:608
  436.0 0.7 copy-start.38
  436.0 3.9 copy-start.25
  436.0 4.0 copy-start.18
  436.0 15.8 %copy-start.17 = (f32[8,768]{1,0:T(8,128)S(1)}, f32[8,768]{1,0:T(8,128)}, u32[]{:S(2)}) copy-start(f32[8,768]{1,0:T(8,128)} %get-tuple-element.54) | copy-start | bytes 73732
  636.5 4.4 copy-start.4
  640.8 3.3 copy-start.3
  644.1 50.4 %copy-start.14 = (f32[1536]{0:T(1024)S(1)}, f32[1536]{0:T(1024)}, u32[]{:S(2)}) copy-start(f32[1536]{0:T(1024)} %param.17) | copy-start | bytes 18436
  (2 other events, 1.2 us)
Sparse Core Ops, SparseCore 0:
  74.5 45.8 all-gather.7
  121.9 45.3 all-gather.5
  235.6 45.3 all-gather.9
  359.3 26.2 reduce-scatter.7
  391.1 243.6 all-reduce.8
  637.1 57.3 reduce-scatter.5
  697.2 59.1 reduce-scatter.3
